TPU v7x, 256 devices: a whole 4x4x8 slice. The times are simulated.
256 devices in a mesh: grid: 16 (over z_hi, y, core), band: 16 (over x, z_lo).
Axes of the slice: x: 4, y: 4, z: 8 (z_hi: 2, z_lo: 4; z = z_hi * 4 + z_lo), core: 2. Of those that a mesh axis runs over, the one named last changes fastest.
Arguments:
- states: bfloat16 [24576, 32768], P('grid', 'band')
- applied: bfloat16 [24576, 32768], P('grid', 'band')
Outputs:
- gram_block: float32 [512, 32768], P('grid', 'band')
- projected: float32 [512, 32768], P('grid', 'band')
All inputs are finite; a program needn't handle non-finite values.
Results may differ from a plain program's by a relative error of at most 0.0003.
Values may be sent and summed in bfloat16 or wider, within the bound.
A program may use at most 64 MiB of HBM per device.

v0:
```python
import jax
import jax.numpy as jnp
from jax import lax
from jax.sharding import PartitionSpec as P

GROUP = 256
STEPS = 2


def passed_along(x, axis, by):
    length = lax.axis_size(axis)
    return lax.ppermute(x, axis, [(i, (i + by) % length) for i in range(length)])


def group_product(group_cols, own):
    return lax.dot_general(
        group_cols, own, (((0,), (0,)), ((), ())), preferred_element_type=jnp.float32
    )


def per_device(states, applied):
    width = states.shape[1]
    received = []
    for s in range(STEPS):
        low_col = s * GROUP
        pair = passed_along(
            (states[:, low_col : low_col + GROUP], applied[:, low_col : low_col + GROUP]),
            "band",
            s + 1,
        )
        received.append(pair)
    all_x = jnp.concatenate([pair[0] for pair in received], axis=1)
    all_h = jnp.concatenate([pair[1] for pair in received], axis=1)
    partial_sum = jnp.concatenate(
        [group_product(all_x, states), group_product(all_h, states)], axis=1
    )
    summed = lax.psum_scatter(partial_sum, "grid", scatter_dimension=0, tiled=True)
    return (summed[:, :width], summed[:, width:])


def solution(mesh):
    in_specs = (P("grid", "band"), P("grid", "band"))
    out_specs = (P("grid", "band"), P("grid", "band"))
    return jax.shard_map(
        per_device, mesh=mesh, in_specs=in_specs, out_specs=out_specs, check_vma=False
    )
```

profile of v0, /device:TPU:1, one launch (start us, length us, event | category | flops | bytes accessed | tf_op | source)
XLA Modules:
  0.0 277.2 jit_solution(11851167129354060008)
XLA Ops:
  7.2 0.0 reduce-scatter.2.cloned.1.call-start
  7.2 0.0 copy-start
  7.2 1.6 fusion.10
  8.9 2.5 collective-permute-start
  11.4 3.0 %collective-permute-start.1 = (bf16[1536,256]{1,0:T(8,128)(2,1)S(1)}, bf16[1536,256]{1,0:T(8,128)(2,1)S(1)}, u32[]{:S(2)}, u32[]{:S(2)}) collective-permute-start(bf16[1536,256]{1,0:T(8,128)(2,1)S(1)} %get-tuple-element.3), channel_id=1, source_target_pairs={{0,2},{1,3},{2,4},{3,5},{4,6},{5,7},{6,8},{7,9},{8,10},{9,11},{10,... | collective-permute-start | bytes 2359304 | tf_op jit(solution)/shard_map/ppermute | solution.py:12
  14.4 1.5 fusion.11
  15.9 0.2 collective-permute-start.2
  16.0 1.8 collective-permute-start.3
  17.9 14.8 %collective-permute-done = bf16[1536,256]{1,0:T(8,128)(2,1)S(1)} collective-permute-done((bf16[1536,256]{1,0:T(8,128)(2,1)S(1)}, bf16[1536,256]{1,0:T(8,128)(2,1)S(1)}, u32[]{:S(2)}, u32[]{:S(2)}) %collective-permute-start) | collective-permute-done | bytes 786464 | tf_op jit(solution)/shard_map/ppermute | solution.py:12
  32.7 69.0 %collective-permute-done.1 = bf16[1536,256]{1,0:T(8,128)(2,1)S(1)} collective-permute-done((bf16[1536,256]{1,0:T(8,128)(2,1)S(1)}, bf16[1536,256]{1,0:T(8,128)(2,1)S(1)}, u32[]{:S(2)}, u32[]{:S(2)}) %collective-permute-start.1) | collective-permute-done | bytes 786464 | tf_op jit(solution)/shard_map/ppermute | solution.py:12
  101.7 0.0 copy-done
  101.7 3.5 %fusion = f32[512,2048]{1,0:T(8,128)S(1)} fusion(bf16[1536,2048]{1,0:T(8,128)(2,1)S(1)} %copy-done, bf16[1536,256]{1,0:T(8,128)(2,1)S(1)} %collective-permute-done.1, bf16[1536,256]{1,0:T(8,128)(2,1)S(1)} %collective-permute-done), kind=kOutput, calls=%fused_computation.1 | convolution fusion | flops 3224371200 | bytes 12058624 | tf_op jit(solution)/shard_map/dot_general | solution.py:16
  105.2 0.0 collective-permute-done.2
  105.2 13.4 %collective-permute-done.3 = bf16[1536,256]{1,0:T(8,128)(2,1)S(1)} collective-permute-done((bf16[1536,256]{1,0:T(8,128)(2,1)S(1)}, bf16[1536,256]{1,0:T(8,128)(2,1)S(1)}, u32[]{:S(2)}, u32[]{:S(2)}) %collective-permute-start.3) | collective-permute-done | bytes 786464 | tf_op jit(solution)/shard_map/ppermute | solution.py:12
  118.6 3.5 %fusion.4 = f32[512,2048]{1,0:T(8,128)S(1)} fusion(bf16[1536,2048]{1,0:T(8,128)(2,1)S(1)} %copy-done, bf16[1536,256]{1,0:T(8,128)(2,1)S(1)} %collective-permute-done.3, bf16[1536,256]{1,0:T(8,128)(2,1)S(1)} %collective-permute-done.2), kind=kOutput, calls=%fused_computation.5 | convolution fusion | flops 3224371200 | bytes 12058624 | tf_op jit(solution)/shard_map/dot_general | solution.py:16
  122.0 3.8 %pad_maximum_fusion = f32[512,4096]{1,0:T(8,128)} fusion(f32[512,2048]{1,0:T(8,128)S(1)} %fusion.4, f32[512,2048]{1,0:T(8,128)S(1)} %fusion), kind=kLoop, calls=%fused_computation | loop fusion | flops 2097152 | bytes 16777216 | tf_op jit(solution)/shard_map/concatenate | solution.py:34
  125.8 0.0 reduce-scatter.2.cloned.1.call-update
  125.8 142.6 %reduce-scatter.2.cloned.1.call-done = f32[32,4096]{1,0:T(8,128)} async-done(((f32[512,4096]{1,0:T(8,128)}), f32[32,4096]{1,0:T(8,128)}) %reduce-scatter.2.cloned.1.call-update) | async-done | bytes 524304 | tf_op jit(solution)/shard_map/reduce_scatter | solution.py:37
  268.5 1.9 fusion.12
Async XLA Ops:
  7.2 261.3 %reduce-scatter.2.cloned.1.call-start = ((), (), s32[]{:S(2)}) async-start(), calls=%async_computation.1 | async-start | bytes 8912896 | tf_op jit(solution)/shard_map/reduce_scatter | solution.py:37
  7.2 94.5 %copy-start = (bf16[1536,2048]{1,0:T(8,128)(2,1)S(1)}, bf16[1536,2048]{1,0:T(8,128)(2,1)}, u32[]{:S(2)}) copy-start(bf16[1536,2048]{1,0:T(8,128)(2,1)} %param.2) | copy-start | bytes 18874372
  8.9 23.8 %collective-permute-start = (bf16[1536,256]{1,0:T(8,128)(2,1)S(1)}, bf16[1536,256]{1,0:T(8,128)(2,1)S(1)}, u32[]{:S(2)}, u32[]{:S(2)}) collective-permute-start(bf16[1536,256]{1,0:T(8,128)(2,1)S(1)} %get-tuple-element.2), channel_id=1, source_target_pairs={{0,1},{1,2},{2,3},{3,4},{4,5},{5,6},{6,7},{7,8},{8,9},{9,10},{10,1... | collective-permute-start | bytes 2359304 | tf_op jit(solution)/shard_map/ppermute | solution.py:12
  11.4 90.3 %collective-permute-start.1 = (bf16[1536,256]{1,0:T(8,128)(2,1)S(1)}, bf16[1536,256]{1,0:T(8,128)(2,1)S(1)}, u32[]{:S(2)}, u32[]{:S(2)}) collective-permute-start(bf16[1536,256]{1,0:T(8,128)(2,1)S(1)} %get-tuple-element.3), channel_id=1, source_target_pairs={{0,2},{1,3},{2,4},{3,5},{4,6},{5,7},{6,8},{7,9},{8,10},{9,11},{10,... | collective-permute-start | bytes 2359304 | tf_op jit(solution)/shard_map/ppermute | solution.py:12
  15.9 89.3 %collective-permute-start.2 = (bf16[1536,256]{1,0:T(8,128)(2,1)S(1)}, bf16[1536,256]{1,0:T(8,128)(2,1)S(1)}, u32[]{:S(2)}, u32[]{:S(2)}) collective-permute-start(bf16[1536,256]{1,0:T(8,128)(2,1)S(1)} %get-tuple-element.4), channel_id=1, source_target_pairs={{0,1},{1,2},{2,3},{3,4},{4,5},{5,6},{6,7},{7,8},{8,9},{9,10},{10,1... | collective-permute-start | bytes 2359304 | tf_op jit(solution)/shard_map/ppermute | solution.py:12
  16.0 102.5 %collective-permute-start.3 = (bf16[1536,256]{1,0:T(8,128)(2,1)S(1)}, bf16[1536,256]{1,0:T(8,128)(2,1)S(1)}, u32[]{:S(2)}, u32[]{:S(2)}) collective-permute-start(bf16[1536,256]{1,0:T(8,128)(2,1)S(1)} %get-tuple-element.5), channel_id=1, source_target_pairs={{0,2},{1,3},{2,4},{3,5},{4,6},{5,7},{6,8},{7,9},{8,10},{9,11},{10,... | collective-permute-start | bytes 2359304 | tf_op jit(solution)/shard_map/ppermute | solution.py:12
Sparse Core Ops, SparseCore 0:
  126.0 142.4 reduce-scatter.1
where the time goes:
time: 278 us; the launch traced here: 277 us
  waiting for transfers between devices  240 us (86%)
  between operations  14.1 us (5%)
  starting transfers between devices  7.59 us (3%)
  matrix products  6.94 us (2%)
  local copies, waits for them, and re-layouts  4.98 us (2%)
  other arithmetic  3.77 us (1%)
    reduce_scatter x1, waiting for transfers between devices, per_device(): lax.psum_scatter(partial_sum, 'grid', scatter_dimension=0, tiled=True)  143 us
    ppermute x4, waiting for transfers between devices, passed_along(): lax.ppermute(x, axis, [(i, (i + by) % length) for i in range(length)])  97.2 us
    ppermute x4, starting transfers between devices, passed_along(): lax.ppermute(x, axis, [(i, (i + by) % length) for i in range(length)])  7.55 us
    dot_general x2, matrix products, group_product(): lax.dot_general(group_cols, own, (((0,), (0,)), ((), ())), preferred_elem...  6.94 us
  transfers between devices with their start and end apart: 5, of which 4 were waited for; matrix products, arithmetic and copies ran while one was open for 2% of the time, Pallas kernels for 0%

commit v1 on v0

v1 whole, which is shorter than its diff:
```python
import jax
import jax.numpy as jnp
from jax import lax
from jax.experimental import pallas as pl
from jax.experimental.pallas import tpu as pltpu
from jax.sharding import PartitionSpec as P

MESH = pl.DeviceIdType.MESH
GROUP = 256
STEPS = 2
N_BAND = 16
N_Y = 4
ROWS = 32
PIECES = 4
KINDS = 2


def kernel(
    x_ref, h_ref, gram_ref, proj_ref,
    own, group, group_t, part, from_core, from_y, away, from_z,
    own_sem, group_send, group_recv, core_send, core_recv, y_send, y_recv, z_send, z_recv,
):
    width = own.shape[1]
    piece = width // PIECES
    grid_at, band_at = lax.axis_index("grid"), lax.axis_index("band")
    half, y_at, core = grid_at // 8, lax.rem(grid_at // 2, N_Y), lax.rem(grid_at, 2)

    def band(by):
        return {"band": lax.rem(band_at + by + N_BAND, N_BAND)}

    def along_y(by):
        return {"grid": half * 8 + lax.rem(y_at + by, N_Y) * 2 + core}

    sibling = {"grid": grid_at + 1 - 2 * core}
    opposite = {"grid": lax.rem(grid_at + 8, 16)}

    load = pltpu.make_async_copy(x_ref, own, own_sem)
    load.start()

    barrier = pltpu.get_barrier_semaphore()
    partners = [band(1), band(-1), band(2), band(-2), sibling, opposite]
    partners += [along_y(k) for k in range(1, N_Y)]
    for partner in partners:
        pl.semaphore_signal(barrier, inc=1, device_id=partner, device_id_type=MESH)
    pl.semaphore_wait(barrier, len(partners))

    def group_copy(chunk):
        step = (1 - half) if chunk < KINDS else half
        source = x_ref if chunk % KINDS == 0 else h_ref
        low = pl.multiple_of(step * GROUP, GROUP)
        return pltpu.make_async_remote_copy(
            src_ref=source.at[:, pl.ds(low, GROUP)],
            dst_ref=group.at[chunk],
            send_sem=group_send.at[chunk],
            recv_sem=group_recv.at[chunk],
            device_id={"band": lax.rem(band_at + step + 1, N_BAND)},
            device_id_type=MESH,
        )

    def core_copy(chunk, p):
        cols = pl.ds(p * piece, piece)
        return pltpu.make_async_remote_copy(
            src_ref=part.at[chunk, 1 - core, :, :, cols],
            dst_ref=from_core.at[chunk, :, :, cols],
            send_sem=core_send.at[chunk, p],
            recv_sem=core_recv.at[chunk, p],
            device_id=sibling,
            device_id_type=MESH,
        )

    def y_copy(chunk, p, by):
        cols = pl.ds(p * piece, piece)
        return pltpu.make_async_remote_copy(
            src_ref=part.at[chunk, core, lax.rem(y_at + by, N_Y), :, cols],
            dst_ref=from_y.at[chunk, by - 1, :, cols],
            send_sem=y_send.at[chunk, p, by - 1],
            recv_sem=y_recv.at[chunk, p, by - 1],
            device_id=along_y(by),
            device_id_type=MESH,
        )

    def z_copy(kind):
        return pltpu.make_async_remote_copy(
            src_ref=away.at[kind],
            dst_ref=from_z.at[kind],
            send_sem=z_send.at[kind],
            recv_sem=z_recv.at[kind],
            device_id=opposite,
            device_id_type=MESH,
        )

    def multiply(chunk, p):
        cols = pl.ds(p * piece, piece)
        product = jnp.dot(group_t[...], own[:, cols], preferred_element_type=jnp.float32)
        for y in range(N_Y):
            for c in range(2):
                low = (2 * y + c) * ROWS
                part[chunk, c, y, :, cols] = product[low : low + ROWS]
        core_copy(chunk, p).start()

    def pair_sum(chunk, p):
        cols = pl.ds(p * piece, piece)
        core_copy(chunk, p).wait_recv()
        part[chunk, core, :, :, cols] = part[chunk, core, :, :, cols] + from_core[chunk, :, :, cols]
        for by in (2, 1, 3):
            y_copy(chunk, p, by).start()

    def products(chunk):
        group_copy(chunk).wait_recv()
        group_t[...] = group[chunk].T
        for p in range(PIECES):
            multiply(chunk, p)
            if p > 0:
                pair_sum(chunk, p - 1)
        pair_sum(chunk, PIECES - 1)

    def y_sum(chunk, p):
        cols = pl.ds(p * piece, piece)
        for by in range(1, N_Y):
            y_copy(chunk, p, by).wait_recv()
        return (
            part[chunk, core, y_at, :, cols]
            + from_y[chunk, 0, :, cols]
            + from_y[chunk, 1, :, cols]
            + from_y[chunk, 2, :, cols]
        )

    def away_sum(chunk):
        for p in range(PIECES):
            away[chunk, :, pl.ds(p * piece, piece)] = y_sum(chunk, p)

    def home_sum(chunk, out_ref):
        for p in range(PIECES):
            out_ref[:, pl.ds(p * piece, piece)] = y_sum(chunk, p)

    def finish(kind, out_ref):
        z_copy(kind).wait_recv()
        out_ref[...] += from_z[kind]

    group_copy(0).start()
    group_copy(1).start()
    load.wait()
    group_copy(0).wait_send()
    group_copy(2).start()
    products(0)
    group_copy(1).wait_send()
    group_copy(3).start()
    products(1)
    away_sum(0)
    away_sum(1)
    group_copy(2).wait_send()
    z_copy(0).start()
    products(2)
    group_copy(3).wait_send()
    z_copy(1).start()
    products(3)
    home_sum(2, gram_ref)
    home_sum(3, proj_ref)
    finish(0, gram_ref)
    finish(1, proj_ref)

    for chunk in range(KINDS * STEPS):
        for p in range(PIECES):
            core_copy(chunk, p).wait_send()
            for by in range(1, N_Y):
                y_copy(chunk, p, by).wait_send()
    for kind in range(KINDS):
        z_copy(kind).wait_send()


def per_device(states, applied):
    points, width = states.shape
    chunks = KINDS * STEPS
    f32, bf16, dma = jnp.float32, jnp.bfloat16, pltpu.SemaphoreType.DMA
    out = jax.ShapeDtypeStruct((ROWS, width), f32)
    return pl.pallas_call(
        kernel,
        out_shape=(out, out),
        in_specs=[pl.BlockSpec(memory_space=pl.ANY)] * 2,
        out_specs=(pl.BlockSpec(memory_space=pltpu.VMEM),) * 2,
        scratch_shapes=[
            pltpu.VMEM((points, width), bf16),
            pltpu.VMEM((chunks, points, GROUP), bf16),
            pltpu.VMEM((GROUP, points), bf16),
            pltpu.VMEM((chunks, 2, N_Y, ROWS, width), f32),
            pltpu.VMEM((chunks, N_Y, ROWS, width), f32),
            pltpu.VMEM((chunks, N_Y - 1, ROWS, width), f32),
            pltpu.VMEM((KINDS, ROWS, width), f32),
            pltpu.VMEM((KINDS, ROWS, width), f32),
            dma,
            dma((chunks,)),
            dma((chunks,)),
            dma((chunks, PIECES)),
            dma((chunks, PIECES)),
            dma((chunks, PIECES, N_Y - 1)),
            dma((chunks, PIECES, N_Y - 1)),
            dma((KINDS,)),
            dma((KINDS,)),
        ],
        cost_estimate=pl.CostEstimate(
            flops=2 * points * width * GROUP * chunks, bytes_accessed=4 * points * width, transcendentals=0
        ),
        compiler_params=pltpu.CompilerParams(
            collective_id=0, has_side_effects=True, vmem_limit_bytes=48 * 2**20
        ),
        name="ritz_blocks",
    )(states, applied)


def solution(mesh):
    in_specs = (P("grid", "band"), P("grid", "band"))
    out_specs = (P("grid", "band"), P("grid", "band"))
    return jax.shard_map(
        per_device, mesh=mesh, in_specs=in_specs, out_specs=out_specs, check_vma=False
    )
```

time: 278 us -> 166 us (0.60)
  waiting for transfers between devices: 240 us -> 0 us
  Pallas kernels: 0 us -> 164 us
  between operations: 14.1 us -> 0.64 us
  starting transfers between devices: 7.59 us -> 0 us
  matrix products: 6.94 us -> 0 us
  other arithmetic: 3.77 us -> 0 us
  local copies, waits for them, and re-layouts: 4.98 us -> 1.41 us
    pallas_call x0 -> x1, Pallas kernels: none -> 164 us  [per_device(): pl.pallas_call(kernel, out_shape=(out, out), in_specs=[pl.BlockSpec(memor...]
    reduce_scatter x1 -> x0, waiting for transfers between devices: 143 us -> none  [per_device(): lax.psum_scatter(partial_sum, 'grid', scatter_dimension=0, tiled=True)]
    ppermute x4 -> x0, waiting for transfers between devices: 97.2 us -> none  [passed_along(): lax.ppermute(x, axis, [(i, (i + by) % length) for i in range(length)])]
    ppermute x4 -> x0, starting transfers between devices: 7.55 us -> none  [passed_along(): lax.ppermute(x, axis, [(i, (i + by) % length) for i in range(length)])]
    dot_general x2 -> x0, matrix products: 6.94 us -> none  [group_product(): lax.dot_general(group_cols, own, (((0,), (0,)), ((), ())), preferred_elem...]
    slice x3 -> x0, local copies, waits for them, and re-layouts: 4.98 us -> none  [the longest x1 1.85 us: per_device(): return (summed[:, :width], summed[:, width:])]
    concatenate x1 -> x0, other arithmetic: 3.77 us -> none  [per_device(): jnp.concatenate([group_product(all_x, states), group_product(all_h, state...]
  transfers between devices with their start and end apart: 5 -> 0, of which waited for: 4 -> 0; matrix products, arithmetic and copies ran while one was open for 2% -> 0% of each run, Pallas kernels for 0% -> 0%
where the time goes in v1:
time: 166 us
  Pallas kernels  164 us (99%)
    pallas_call x1, Pallas kernels, per_device(): pl.pallas_call(kernel, out_shape=(out, out), in_specs=[pl.BlockSpec(memor...  164 us

profile of v1, /device:TPU:1, one launch (start us, length us, event | category | flops | bytes accessed | tf_op | source)
XLA Modules:
  0.0 165.9 jit_solution(11563407445658293327)
XLA Ops:
  0.6 163.8 %ritz_blocks.1 = (f32[32,2048]{1,0:T(8,128)S(1)}, f32[32,2048]{1,0:T(8,128)S(1)}) custom-call(bf16[1536,2048]{1,0:T(8,128)(2,1)} %x_ref.1, bf16[1536,2048]{1,0:T(8,128)(2,1)} %h_ref.1), custom_call_target="tpu_custom_call" | custom-call | flops 6442450944 | bytes 12582912 | tf_op jit(solution)/shard_map/ritz_blocks/pallas_call | solution.py:176
  164.5 0.7 copy.6
  165.2 0.7 copy.7
